TPU v7x, 768 devices: a whole 4x8x12 slice. The times are simulated.
768 devices in a mesh: dom: 192 (over z, y, core), grp: 4 (over x).
Axes of the slice: x: 4, y: 8, z: 12, core: 2. Of those that a mesh axis runs over, the one named last changes fastest.
Arguments:
- features: bfloat16 [393216, 512], P(('dom', 'grp')), may hold values from -6 to 6
- halo_in: bfloat16 [393216, 512], P(('dom', 'grp')), may hold values from -6 to 6
- neighbors: int32 [393216, 10], P(('dom', 'grp')), may hold values from 0 to 1023
- send_rows: int32 [393216], P(('dom', 'grp')), may hold values from 0 to 511
- grad_halo_in: bfloat16 [393216, 512], P(('dom', 'grp')), may hold values from -6 to 6
- out_grad: bfloat16 [393216, 512], P(('dom', 'grp')), may hold values from -6 to 6
- w_self: bfloat16 [512, 512], replicated, may hold values from -0.25 to 0.25
- w_neigh: bfloat16 [512, 512], replicated, may hold values from -0.25 to 0.25
Outputs:
- layer_out: bfloat16 [393216, 512], P(('dom', 'grp'))
- feat_grad: bfloat16 [393216, 512], P(('dom', 'grp'))
- next_halo: bfloat16 [393216, 512], P(('dom', 'grp'))
- next_grad_halo: bfloat16 [393216, 512], P(('dom', 'grp'))
- w_grads: float32 [2, 512, 512], replicated
Inputs may be any that keep to these rules, and one draw needn't show every extreme that they name: `neighbors`: each entry names one of its partition's 512 own rows or 512 halo rows. `send_rows`: each entry names one of its partition's own rows.
All inputs are finite; a program needn't handle non-finite values.
Results may differ from a plain program's by a relative error of at most 0.005.
Values may be sent and summed in bfloat16 or wider, within the bound.
A program may use at most 32 MiB of HBM per device.

v0:
```python
import math

import jax
import jax.numpy as jnp
from jax import lax
from jax.sharding import PartitionSpec as P


def body(features, halo_in, neighbors, send_rows, grad_halo_in, out_grad, w_self, w_neigh):
    local_rows = features.shape[0]
    halo_rows = halo_in.shape[0]
    fanout = neighbors.shape[1]
    sent_rows = jnp.take(features, send_rows, axis=0)
    next_halo = lax.all_to_all(sent_rows, "grp", split_axis=0, concat_axis=0, tiled=True)
    row_table = jnp.concatenate([features, halo_in], axis=0)
    table_ids = lax.broadcasted_iota(jnp.int32, (1, local_rows + halo_rows), 1)
    counts = jnp.zeros((local_rows, local_rows + halo_rows), jnp.float32)
    for slot in range(fanout):
        counts = counts + (neighbors[:, slot : slot + 1] == table_ids).astype(jnp.float32)
    counts_half = counts.astype(jnp.bfloat16)
    aggregate = (
        jnp.dot(counts_half, row_table, preferred_element_type=jnp.float32) / fanout
    ).astype(jnp.bfloat16)
    pre_act = jnp.dot(features, w_self, preferred_element_type=jnp.float32) + jnp.dot(
        aggregate, w_neigh, preferred_element_type=jnp.float32
    )
    sigmoid = jax.nn.sigmoid(pre_act)
    layer_out = (pre_act * sigmoid).astype(jnp.bfloat16)
    act_grad = (out_grad.astype(jnp.float32) * sigmoid * (1.0 + pre_act * (1.0 - sigmoid))).astype(
        jnp.bfloat16
    )
    contract_rows = (((0,), (0,)), ((), ()))
    contract_cols = (((1,), (1,)), ((), ()))
    wself_grad = lax.dot_general(
        features, act_grad, contract_rows, preferred_element_type=jnp.float32
    )
    wneigh_grad = lax.dot_general(
        aggregate, act_grad, contract_rows, preferred_element_type=jnp.float32
    )
    self_grad = lax.dot_general(act_grad, w_self, contract_cols, preferred_element_type=jnp.float32)
    neigh_grad = (
        lax.dot_general(act_grad, w_neigh, contract_cols, preferred_element_type=jnp.float32)
        / fanout
    )
    table_grad = lax.dot_general(
        counts,
        neigh_grad,
        contract_rows,
        precision=lax.Precision.HIGHEST,
        preferred_element_type=jnp.float32,
    )
    own_ids = lax.broadcasted_iota(jnp.int32, (1, local_rows), 1)
    select = (send_rows[:, None] == own_ids).astype(jnp.bfloat16)
    returned = lax.dot_general(
        select, grad_halo_in, contract_rows, preferred_element_type=jnp.float32
    )
    feat_grad = (self_grad + (table_grad[:local_rows] + returned)).astype(jnp.bfloat16)
    halo_grad = table_grad[local_rows:].astype(jnp.bfloat16)
    next_grad_halo = lax.all_to_all(halo_grad, "grp", split_axis=0, concat_axis=0, tiled=True)
    weight_terms = jnp.stack([wself_grad, wneigh_grad])
    summed = lax.psum(weight_terms, ("dom", "grp"))
    total_nodes = local_rows * lax.axis_size("dom") * lax.axis_size("grp")
    grad_scale = 1.0 / math.sqrt(total_nodes)
    w_grads = summed * grad_scale
    return (layer_out, feat_grad, next_halo, next_grad_halo, w_grads)


def solution(mesh):
    return jax.shard_map(
        body,
        mesh=mesh,
        in_specs=(
            P(("dom", "grp"), None),
            P(("dom", "grp"), None),
            P(("dom", "grp"), None),
            P(("dom", "grp")),
            P(("dom", "grp"), None),
            P(("dom", "grp"), None),
            P(),
            P(),
        ),
        out_specs=(
            P(("dom", "grp"), None),
            P(("dom", "grp"), None),
            P(("dom", "grp"), None),
            P(("dom", "grp"), None),
            P(),
        ),
        check_vma=False,
    )
```

profile of v0, /device:TPU:1, one launch (start us, length us, event | category | flops | bytes accessed | tf_op | source)
XLA Modules:
  0.0 521.0 jit_solution(2150876062935278503)
XLA Ops:
  7.2 0.0 copy-start
  7.2 0.7 compare_select_fusion
  7.9 0.7 and_bitcast_fusion
  8.6 3.1 gather_fusion
  11.7 0.0 copy-start.1
  11.7 0.0 copy-start.3
  11.7 0.0 copy-start.8
  11.8 0.0 copy-start.9
  11.8 0.9 broadcast_select_fusion
  12.7 4.8 all-to-all-start
  17.5 0.0 all-reduce.2.cloned.1.call-start
  17.6 0.0 copy-done.1
  17.6 0.0 copy-done.3
  17.6 0.4 fusion.11
  18.0 0.0 copy-done.8
  18.0 0.0 copy-done.9
  18.0 0.0 copy-start.10
  18.1 2.8 fusion.1
  20.9 0.0 copy-done
  20.9 0.0 copy-done.10
  20.9 1.6 multiply_convert_fusion
  22.5 0.5 convolution_bitcast_fusion
  23.0 0.5 convolution_bitcast_fusion.1
  23.5 1.5 pad_maximum_fusion
  25.0 0.0 all-reduce.2.cloned.1.call-update
  25.0 0.5 convolution_multiply_fusion
  25.5 6.1 %fusion.7 = f32[1024,512]{1,0:T(8,128)S(1)} fusion(f32[512,512]{1,0:T(8,128)S(1)} %convolution_multiply_fusion, s32[512]{0:T(512)S(1)} %bitcast.56, s32[512]{0:T(512)S(1)} %bitcast.58, s32[512]{0:T(512)S(1)} %bitcast.42, s32[512]{0:T(512)S(1)} %bitcast.44, s32[512]{0:T(512)S(1)} %bitcast.46, s32[512]{0:T(512)S(1)} %bitcast.48, s32[512]{0:T(512)S(1)} %bitcast.50, ...), kind=kOutput, calls=%fused_computation.32 | convolution fusion | flops 3236429824 | bytes 3166208 | tf_op jit(solution)/shard_map/dot_general | solution.py:45
  31.6 0.0 copy-start.4
  31.6 1.3 copy-done.4
  32.9 0.0 copy-start.6
  32.9 0.0 copy-start.7
  32.9 0.9 slice.55
  33.7 0.0 all-to-all-done
  33.7 4.2 all-to-all-start.1
  38.0 0.0 copy-start.5
  38.0 0.5 fusion.12
  38.4 0.0 copy-done.6
  38.5 0.0 copy-done.7
  38.5 1.1 copy-done.5
  39.6 1.4 fusion.2
  40.9 4.0 all-to-all-done.1
  44.9 0.0 copy-start.2
  44.9 0.8 copy-done.2
  45.7 462.1 %all-reduce.2.cloned.1.call-done = f32[2,512,512]{1,2,0:T(8,128)} async-done(((f32[2,512,512]{1,2,0:T(8,128)}), f32[2,512,512]{1,2,0:T(8,128)}) %all-reduce.2.cloned.1.call-update) | async-done | bytes 2097168 | tf_op jit(solution)/shard_map/psum | solution.py:61
  507.8 1.8 broadcast_multiply_fusion
  509.7 1.8 copy.14
  511.5 0.8 copy.19
  512.3 1.9 copy.20
  (2 shorter events, 0.0 us)
Async XLA Ops:
  7.2 13.7 %copy-start = (bf16[512,512]{1,0:T(8,128)(2,1)S(1)}, bf16[512,512]{1,0:T(8,128)(2,1)}, u32[]{:S(2)}) copy-start(bf16[512,512]{1,0:T(8,128)(2,1)} %param.15) | copy-start | bytes 1572868
  11.7 5.8 %copy-start.1 = (bf16[512,512]{1,0:T(8,128)(2,1)S(1)}, bf16[512,512]{1,0:T(8,128)(2,1)}, u32[]{:S(2)}) copy-start(bf16[512,512]{1,0:T(8,128)(2,1)} %param.8) | copy-start | bytes 1572868
  11.7 5.8 %copy-start.3 = (bf16[512,512]{1,0:T(8,128)(2,1)S(1)}, bf16[512,512]{1,0:T(8,128)(2,1)}, u32[]{:S(2)}) copy-start(bf16[512,512]{1,0:T(8,128)(2,1)} %param.14) | copy-start | bytes 1572868
  11.7 6.2 %copy-start.8 = (s32[512,10]{0,1:T(8,128)S(1)}, s32[512,10]{0,1:T(8,128)}, u32[]{:S(2)}) copy-start(s32[512,10]{0,1:T(8,128)} %param.10) | copy-start | bytes 61444
  11.8 6.3 %copy-start.9 = (bf16[512,512]{1,0:T(8,128)(2,1)S(1)}, bf16[512,512]{1,0:T(8,128)(2,1)}, u32[]{:S(2)}) copy-start(bf16[512,512]{1,0:T(8,128)(2,1)} %param.9) | copy-start | bytes 1572868
  12.7 21.0 %all-to-all-start = ((bf16[4,128,512]{2,1,0:T(8,128)(2,1)}), bf16[4,128,512]{2,1,0:T(8,128)(2,1)S(1)}, u32[]{:S(2)}, u32[]{:S(2)}) async-start(bf16[4,128,512]{2,1,0:T(8,128)(2,1)} %broadcast_select_fusion), calls=%async_computation | async-start | bytes 1048576 | tf_op jit(solution)/shard_map/all_to_all | solution.py:14
  17.5 490.3 %all-reduce.2.cloned.1.call-start = ((), (), s32[]{:S(2)}) async-start(), calls=%async_computation.2 | async-start | bytes 4194304 | tf_op jit(solution)/shard_map/psum | solution.py:61
  18.0 2.8 copy-start.10
  31.6 1.3 copy-start.4
  32.9 5.6 %copy-start.6 = (bf16[512,512]{1,0:T(8,128)(2,1)S(1)}, bf16[512,512]{1,0:T(8,128)(2,1)}, u32[]{:S(2)}) copy-start(bf16[512,512]{1,0:T(8,128)(2,1)} %param.12) | copy-start | bytes 1572868
  32.9 5.6 %copy-start.7 = (s32[512]{0:T(512)S(1)}, s32[512]{0:T(512)}, u32[]{:S(2)}) copy-start(s32[512]{0:T(512)} %param.11) | copy-start | bytes 6148
  33.7 11.2 %all-to-all-start.1 = ((bf16[4,128,512]{2,1,0:T(8,128)(2,1)}), bf16[4,128,512]{2,1,0:T(8,128)(2,1)S(1)}, u32[]{:S(2)}, u32[]{:S(2)}) async-start(bf16[4,128,512]{2,1,0:T(8,128)(2,1)} %bitcast.13), calls=%async_computation.1 | async-start | bytes 1048576 | tf_op jit(solution)/shard_map/all_to_all | solution.py:59
  38.0 1.6 copy-start.5
  44.9 0.8 copy-start.2
Sparse Core Ops, SparseCore 0:
  25.1 482.6 all-reduce.1
where the time goes:
time: 523 us; the launch traced here: 521 us
  waiting for transfers between devices  466 us (89%)
  matrix products  14.2 us (3%)
  between operations  14.2 us (3%)
  local copies, waits for them, and re-layouts  11.7 us (2%)
  starting transfers between devices  9.08 us (2%)
  other arithmetic  5.7 us (1%)
    psum x1, waiting for transfers between devices, body(): summed = lax.psum(weight_terms, ('dom', 'grp'))  462 us
  transfers between devices with their start and end apart: 3, of which 2 were waited for; matrix products, arithmetic and copies ran while one was open for 3% of the time, Pallas kernels for 0%

commit v1 on v0

v1 whole, which is shorter than its diff:
```python
import functools
import math

import jax
import jax.numpy as jnp
from jax import lax
from jax.experimental import pallas as pl
from jax.experimental.pallas import tpu as pltpu
from jax.sharding import PartitionSpec as P

MESH = pl.DeviceIdType.MESH
NX, NY, NZ = 4, 8, 12
ROWS = 512
H = 512
FAN = 10
XB = ROWS // NX
YB = XB // NY
CH = 4
CW = H // CH
DIM0 = (((0,), (0,)), ((), ()))
DIM1 = (((1,), (1,)), ((), ()))
F32 = jnp.float32
BF16 = jnp.bfloat16


def kernel(
    scale,
    feat_hbm, halo_hbm, nbr_hbm, send_hbm, gin_hbm, ograd_hbm, ws_hbm, wn_hbm,
    layer_hbm, fgrad_hbm, nhalo_hbm, nghalo_hbm, wout_hbm,
    table, pair, nbr, send, gin, ograd, wself, wneigh,
    counts, select, act, layer, fgrad, hgrad, sent,
    wpart, crecv, s1, xsend, xrecv, s2, ysend, yrecv, zbuf, ag,
    lsem, osem, cs, cr, xs, xr, ys, yr, zs, zr, ays, ayr, axs, axr, acs, acr, hs, hr, gs, gr,
):
    dom = lax.axis_index("dom")
    g = lax.axis_index("grp")
    core = lax.rem(dom, 2)
    y = lax.rem(dom // 2, NY)
    z = dom // (2 * NY)

    def at_core():
        return (dom + 1 - 2 * core, g)

    def at_x(k):
        return (dom, lax.rem(g + k, NX))

    def at_y(k):
        return ((z * NY + lax.rem(y + k, NY)) * 2 + core, g)

    def at_z(k):
        return ((lax.rem(z + k, NZ) * NY + y) * 2 + core, g)

    barrier = pltpu.get_barrier_semaphore()
    peers = [at_core()] + [at_x(k) for k in range(1, NX)]
    peers += [at_y(k) for k in range(1, NY)] + [at_z(k) for k in range(1, NZ)]
    for peer in peers:
        pl.semaphore_signal(barrier, inc=1, device_id=peer, device_id_type=MESH)

    loads = [
        (nbr_hbm, nbr),
        (feat_hbm, table.at[pl.ds(0, ROWS)]),
        (halo_hbm, table.at[pl.ds(ROWS, ROWS)]),
        (ws_hbm, wself),
        (wn_hbm, wneigh),
        (ograd_hbm, ograd),
        (feat_hbm, pair.at[0]),
        (send_hbm, send),
        (gin_hbm, gin),
    ]
    copies = [pltpu.make_async_copy(s, d, lsem.at[i]) for i, (s, d) in enumerate(loads)]
    for copy in copies:
        copy.start()

    copies[0].wait()
    RB = 64
    ids = lax.broadcasted_iota(jnp.int32, (RB, 2 * ROWS), 1)

    @pl.loop(0, ROWS // RB)
    def _(b):
        rows = pl.ds(pl.multiple_of(b * RB, RB), RB)
        block = nbr[rows, :]
        total = jnp.zeros((RB, 2 * ROWS), F32)
        for slot in range(FAN):
            total = total + jnp.where(block[:, slot : slot + 1] == ids, 1.0, 0.0)
        counts[rows, :] = total.astype(BF16)

    for i in (1, 2, 3, 4, 5, 6):
        copies[i].wait()
    agg = jnp.dot(counts[...], table[...], preferred_element_type=F32) * (1.0 / FAN)
    pair[1] = agg.astype(BF16)
    pre = jnp.dot(table[pl.ds(0, ROWS), :], wself[...], preferred_element_type=F32)
    pre = pre + jnp.dot(pair[1], wneigh[...], preferred_element_type=F32)
    sig = jax.nn.sigmoid(pre)
    layer[...] = (pre * sig).astype(BF16)
    act[...] = (ograd[...].astype(F32) * sig * (1.0 + pre * (1.0 - sig))).astype(BF16)

    mine = core * ROWS
    other = ROWS - mine

    def cols(c):
        return pl.ds(c * CW, CW)

    def remote(src, dst, send_sem, recv_sem, device):
        copy = pltpu.make_async_remote_copy(
            src_ref=src, dst_ref=dst, send_sem=send_sem, recv_sem=recv_sem,
            device_id=device, device_id_type=MESH,
        )
        copy.start()

    def wait_for(ref, sem):
        pltpu.make_async_copy(ref, ref, sem).wait()

    wpart[1] = lax.dot_general(pair[1 - core], act[...], DIM0, preferred_element_type=F32)
    pl.semaphore_wait(barrier, len(peers))
    for c in range(CH):
        remote(wpart.at[1, :, cols(c)], crecv.at[:, cols(c)], cs.at[c], cr.at[c], at_core())
    wpart[0] = lax.dot_general(pair[core], act[...], DIM0, preferred_element_type=F32)
    out_layer = pltpu.make_async_copy(layer, layer_hbm, osem.at[0])
    out_layer.start()

    for c in range(CH):
        wait_for(crecv.at[:, cols(c)], cr.at[c])
        total = wpart[0, :, cols(c)] + crecv[:, cols(c)]
        s1[:, cols(c)] = total
        xsend[:, cols(c)] = total.astype(BF16)
        for k in range(1, NX):
            to = lax.rem(g + k, NX)
            rows = pl.ds(pl.multiple_of(to * XB, XB), XB)
            remote(xsend.at[rows, cols(c)], xrecv.at[c, k - 1], xs.at[c], xr.at[c], at_x(k))

    copies[7].wait()
    copies[8].wait()
    own_ids = lax.broadcasted_iota(jnp.int32, (ROWS, ROWS), 0)
    select[...] = jnp.where(own_ids == send[...], 1.0, 0.0).astype(BF16)
    sent[...] = lax.dot_general(
        select[...], table[pl.ds(0, ROWS), :], DIM0, preferred_element_type=F32
    ).astype(BF16)
    here = pl.ds(pl.multiple_of(g * XB, XB), XB)
    for k in range(1, NX):
        to = lax.rem(g + k, NX)
        rows = pl.ds(pl.multiple_of(to * XB, XB), XB)
        remote(sent.at[rows], nhalo_hbm.at[here], hs, hr, at_x(k))
    own_sent = pltpu.make_async_copy(sent.at[here], nhalo_hbm.at[here], osem.at[1])
    own_sent.start()

    for c in range(CH):
        wait_for(xrecv.at[c], xr.at[c])
        total = s1[here, cols(c)]
        for k in range(NX - 1):
            total = total + xrecv[c, k].astype(F32)
        s2[:, cols(c)] = total
        ysend[:, cols(c)] = total.astype(BF16)
        for k in range(1, NY):
            to = lax.rem(y + k, NY)
            rows = pl.ds(pl.multiple_of(to * YB, YB), YB)
            remote(
                ysend.at[rows, cols(c)], yrecv.at[c, pl.ds((k - 1) * YB, YB)],
                ys.at[c], yr.at[c], at_y(k),
            )

    grad = lax.dot_general(act[...], wneigh[...], DIM1, preferred_element_type=F32)
    grad = grad * (1.0 / FAN)
    high = grad.astype(BF16)
    low = (grad - high.astype(F32)).astype(BF16)
    back = lax.dot_general(
        counts[:, pl.ds(ROWS, ROWS)], high, DIM0, preferred_element_type=F32
    ) + lax.dot_general(counts[:, pl.ds(ROWS, ROWS)], low, DIM0, preferred_element_type=F32)
    hgrad[...] = back.astype(BF16)
    for k in range(1, NX):
        to = lax.rem(g + k, NX)
        rows = pl.ds(pl.multiple_of(to * XB, XB), XB)
        remote(hgrad.at[rows], nghalo_hbm.at[here], gs, gr, at_x(k))
    own_grad = pltpu.make_async_copy(hgrad.at[here], nghalo_hbm.at[here], osem.at[2])
    own_grad.start()

    own_y = pl.ds(pl.multiple_of(y * YB, YB), YB)
    own_z = pl.ds(pl.multiple_of(z * YB, YB), YB)
    for c in range(CH):
        wait_for(yrecv.at[c], yr.at[c])
        total = s2[own_y, cols(c)]
        for k in range(NY - 1):
            total = total + yrecv[c, pl.ds(k * YB, YB), :].astype(F32)
        zbuf[c, own_z, :] = total.astype(BF16)
        for k in range(1, NZ):
            remote(zbuf.at[c, own_z], zbuf.at[c, own_z], zs.at[c], zr.at[c], at_z(k))

    own = lax.dot_general(act[...], wself[...], DIM1, preferred_element_type=F32)
    own = own + lax.dot_general(
        counts[:, pl.ds(0, ROWS)], high, DIM0, preferred_element_type=F32
    )
    own = own + lax.dot_general(
        counts[:, pl.ds(0, ROWS)], low, DIM0, preferred_element_type=F32
    )
    own = own + jnp.dot(select[...], gin[...], preferred_element_type=F32)
    fgrad[...] = own.astype(BF16)
    out_fgrad = pltpu.make_async_copy(fgrad, fgrad_hbm, osem.at[3])
    out_fgrad.start()

    row_y = pl.ds(pl.multiple_of(mine + g * XB + y * YB, YB), YB)
    row_x = pl.ds(pl.multiple_of(mine + g * XB, XB), XB)
    row_c = pl.ds(pl.multiple_of(mine, ROWS), ROWS)
    row_o = pl.ds(pl.multiple_of(other, ROWS), ROWS)
    for c in range(CH):
        wait_for(zbuf.at[c, pl.ds(0, (NZ - 1) * YB)], zr.at[c])
        total = zbuf[c, pl.ds(0, YB), :].astype(F32)
        for k in range(1, NZ):
            total = total + zbuf[c, pl.ds(k * YB, YB), :].astype(F32)
        ag[row_y, cols(c)] = (total * scale).astype(BF16)
        for k in range(1, NY):
            remote(
                ag.at[row_y, cols(c)], ag.at[row_y, cols(c)], ays.at[c], ayr.at[c], at_y(k)
            )
    for c in range(CH):
        wait_for(ag.at[pl.ds(0, (NY - 1) * YB), cols(c)], ayr.at[c])
        for k in range(1, NX):
            remote(
                ag.at[row_x, cols(c)], ag.at[row_x, cols(c)], axs.at[c], axr.at[c], at_x(k)
            )
    for c in range(CH):
        wait_for(ag.at[pl.ds(0, (NX - 1) * XB), cols(c)], axr.at[c])
        remote(ag.at[row_c, cols(c)], ag.at[row_c, cols(c)], acs.at[c], acr.at[c], at_core())
    out_mine = pltpu.make_async_copy(ag.at[row_c], wout_hbm.at[row_c], osem.at[4])
    out_mine.start()
    for c in range(CH):
        wait_for(ag.at[row_o, cols(c)], acr.at[c])
    out_other = pltpu.make_async_copy(ag.at[row_o], wout_hbm.at[row_o], osem.at[5])
    out_other.start()

    wait_for(nhalo_hbm.at[pl.ds(0, ROWS - XB)], hr)
    wait_for(nghalo_hbm.at[pl.ds(0, ROWS - XB)], gr)
    wait_for(sent.at[pl.ds(0, ROWS - XB)], hs)
    wait_for(hgrad.at[pl.ds(0, ROWS - XB)], gs)
    for c in range(CH):
        wait_for(crecv.at[:, cols(c)], cs.at[c])
        wait_for(xrecv.at[c], xs.at[c])
        wait_for(yrecv.at[c], ys.at[c])
        wait_for(zbuf.at[c, pl.ds(0, (NZ - 1) * YB)], zs.at[c])
        wait_for(ag.at[pl.ds(0, (NY - 1) * YB), cols(c)], ays.at[c])
        wait_for(ag.at[pl.ds(0, (NX - 1) * XB), cols(c)], axs.at[c])
        wait_for(ag.at[row_c, cols(c)], acs.at[c])
    for copy in (out_layer, own_sent, own_grad, out_fgrad, out_mine, out_other):
        copy.wait()


def body(features, halo_in, neighbors, send_rows, grad_halo_in, out_grad, w_self, w_neigh):
    total_nodes = ROWS * lax.axis_size("dom") * lax.axis_size("grp")
    scale = 1.0 / math.sqrt(total_nodes)
    rows = jax.ShapeDtypeStruct((ROWS, H), BF16)
    anywhere = pl.BlockSpec(memory_space=pl.ANY)
    half = pltpu.VMEM((ROWS, H), BF16)
    dma = pltpu.SemaphoreType.DMA
    layer_out, feat_grad, next_halo, next_grad_halo, weights = pl.pallas_call(
        functools.partial(kernel, scale),
        out_shape=(rows, rows, rows, rows, jax.ShapeDtypeStruct((2 * ROWS, H), BF16)),
        in_specs=[anywhere] * 8,
        out_specs=(anywhere,) * 5,
        scratch_shapes=[
            pltpu.VMEM((2 * ROWS, H), BF16),
            pltpu.VMEM((2, ROWS, H), BF16),
            pltpu.VMEM((ROWS, FAN), jnp.int32),
            pltpu.VMEM((1, ROWS), jnp.int32),
            half, half, half, half,
            pltpu.VMEM((ROWS, 2 * ROWS), BF16),
            half, half, half, half, half, half,
            pltpu.VMEM((2, ROWS, H), F32),
            pltpu.VMEM((ROWS, H), F32),
            pltpu.VMEM((ROWS, H), F32),
            half,
            pltpu.VMEM((CH, NX - 1, XB, CW), BF16),
            pltpu.VMEM((XB, H), F32),
            pltpu.VMEM((XB, H), BF16),
            pltpu.VMEM((CH, (NY - 1) * YB, CW), BF16),
            pltpu.VMEM((CH, NZ * YB, CW), BF16),
            pltpu.VMEM((2 * ROWS, H), BF16),
            dma((9,)), dma((6,)),
        ] + [dma((CH,))] * 14 + [dma] * 4,
        compiler_params=pltpu.CompilerParams(
            collective_id=0, has_side_effects=True, vmem_limit_bytes=48 << 20
        ),
    )(
        features, halo_in, neighbors, send_rows.reshape(1, ROWS), grad_halo_in, out_grad,
        w_self, w_neigh,
    )
    w_grads = weights.astype(F32).reshape(2, ROWS, H)
    return layer_out, feat_grad, next_halo, next_grad_halo, w_grads


def solution(mesh):
    rows = P(("dom", "grp"), None)
    return jax.shard_map(
        body,
        mesh=mesh,
        in_specs=(rows, rows, rows, P(("dom", "grp")), rows, rows, P(), P()),
        out_specs=(rows, rows, rows, rows, P()),
        check_vma=False,
    )
```

time: 523 us -> 69.4 us (0.13)
  waiting for transfers between devices: 466 us -> 0 us
  Pallas kernels: 0 us -> 54.4 us
  matrix products: 14.2 us -> 0 us
  between operations: 14.2 us -> 0.66 us
  starting transfers between devices: 9.08 us -> 0 us
    psum x1 -> x0, waiting for transfers between devices: 462 us -> none  [body(): summed = lax.psum(weight_terms, ('dom', 'grp'))]
    pallas_call x0 -> x1, Pallas kernels: none -> 54.4 us  [body(): pl.pallas_call(functools.partial(kernel, scale), out_shape=(rows, rows, r...]
    dot_general x9 -> x0, matrix products: 14.2 us -> none  [the longest x1 6.07 us: body(): lax.dot_general(counts, neigh_grad, contract_rows, precision=lax.Precisio...]
    all_to_all x2 -> x0, starting transfers between devices: 9.08 us -> none  [the longest x1 4.84 us: body(): lax.all_to_all(sent_rows, 'grp', split_axis=0, concat_axis=0, tiled=True)]
    unnamed x25 -> x19, local copies, waits for them, and re-layouts: 7.73 us -> 11 us
  transfers between devices with their start and end apart: 3 -> 0, of which waited for: 2 -> 0; matrix products, arithmetic and copies ran while one was open for 3% -> 0% of each run, Pallas kernels for 0% -> 0%
where the time goes in v1:
time: 69.4 us; the launch traced here: 68.9 us
  Pallas kernels  54.4 us (78%)
  local copies, waits for them, and re-layouts  11 us (16%)
  other arithmetic  2.84 us (4%)
    pallas_call x1, Pallas kernels, body(): pl.pallas_call(functools.partial(kernel, scale), out_shape=(rows, rows, r...  54.4 us
    unnamed x19, local copies, waits for them, and re-layouts  11 us
    reshape x1, other arithmetic, body(): w_grads = weights.astype(F32).reshape(2, ROWS, H)  2.84 us

profile of v1, /device:TPU:1, one launch (start us, length us, event | category | flops | bytes accessed | tf_op | source)
XLA Modules:
  0.0 68.9 jit_solution(2747162787379107332)
XLA Ops:
  0.6 0.9 %copy.13.nbr_hbm = s32[512,10]{1,0:T(8,128)S(1)} copy(s32[512,10]{0,1:T(8,128)} %param.10) | data formatting | bytes 40960 | tf_op args[2]
  1.5 0.0 copy-start
  1.5 1.0 %copy-done = bf16[512,512]{1,0:T(8,128)(2,1)S(1)} copy-done((bf16[512,512]{1,0:T(8,128)(2,1)S(1)}, bf16[512,512]{1,0:T(8,128)(2,1)}, u32[]{:S(2)}) %copy-start) | copy-done | bytes 524312
  2.6 0.0 copy-start.1
  2.6 1.0 %copy-done.1 = bf16[512,512]{1,0:T(8,128)(2,1)S(1)} copy-done((bf16[512,512]{1,0:T(8,128)(2,1)S(1)}, bf16[512,512]{1,0:T(8,128)(2,1)}, u32[]{:S(2)}) %copy-start.1) | copy-done | bytes 524312
  3.6 0.0 copy-start.2
  3.6 1.0 %copy-done.2 = bf16[512,512]{1,0:T(8,128)(2,1)S(1)} copy-done((bf16[512,512]{1,0:T(8,128)(2,1)S(1)}, bf16[512,512]{1,0:T(8,128)(2,1)}, u32[]{:S(2)}) %copy-start.2) | copy-done | bytes 524312
  4.7 0.0 copy-start.3
  4.7 1.0 %copy-done.3 = bf16[512,512]{1,0:T(8,128)(2,1)S(1)} copy-done((bf16[512,512]{1,0:T(8,128)(2,1)S(1)}, bf16[512,512]{1,0:T(8,128)(2,1)}, u32[]{:S(2)}) %copy-start.3) | copy-done | bytes 524312
  5.7 0.0 copy-start.4
  5.7 1.0 %copy-done.4 = bf16[512,512]{1,0:T(8,128)(2,1)S(1)} copy-done((bf16[512,512]{1,0:T(8,128)(2,1)S(1)}, bf16[512,512]{1,0:T(8,128)(2,1)}, u32[]{:S(2)}) %copy-start.4) | copy-done | bytes 524312
  6.7 0.0 copy-start.5
  6.7 1.0 %copy-done.5 = bf16[512,512]{1,0:T(8,128)(2,1)S(1)} copy-done((bf16[512,512]{1,0:T(8,128)(2,1)S(1)}, bf16[512,512]{1,0:T(8,128)(2,1)}, u32[]{:S(2)}) %copy-start.5) | copy-done | bytes 524312
  7.8 0.0 copy-start.6
  7.8 0.7 copy-done.6
  8.5 54.4 %shard_map.119 = (bf16[512,512]{1,0:T(8,128)(2,1)S(1)}, bf16[512,512]{1,0:T(8,128)(2,1)S(1)}, bf16[512,512]{1,0:T(8,128)(2,1)S(1)}, bf16[512,512]{1,0:T(8,128)(2,1)S(1)}, bf16[1024,512]{1,0:T(8,128)(2,1)}) custom-call(bf16[512,512]{1,0:T(8,128)(2,1)S(1)} %copy-done, bf16[512,512]{1,0:T(8,128)(2,1)S(1)} %copy-done.1, s32[512,10]{1,0:T(8,128)S(1)} %copy.13.nbr_hbm, ...), custom_call_target="tpu_custom_call" | custom-call | tf_op jit(solution)/shard_map/pallas_call | solution.py:252
  62.9 2.8 %convert.1 = f32[2,512,512]{2,1,0:T(8,128)} convert(bf16[2,512,512]{2,1,0:T(8,128)(2,1)} %bitcast.4) | non-fusion elementwise | flops 524288 | bytes 3145728 | tf_op jit(solution)/shard_map/reshape | solution.py:284
  65.7 0.8 %copy.18 = bf16[512,512]{1,0:T(8,128)(2,1)} copy(bf16[512,512]{1,0:T(8,128)(2,1)S(1)} %get-tuple-element.20) | data formatting | bytes 1048576
  66.5 0.8 %copy.19 = bf16[512,512]{1,0:T(8,128)(2,1)} copy(bf16[512,512]{1,0:T(8,128)(2,1)S(1)} %get-tuple-element.21) | data formatting | bytes 1048576
  67.3 0.8 %copy.20 = bf16[512,512]{1,0:T(8,128)(2,1)} copy(bf16[512,512]{1,0:T(8,128)(2,1)S(1)} %get-tuple-element.22) | data formatting | bytes 1048576
  68.1 0.8 %copy.21 = bf16[512,512]{1,0:T(8,128)(2,1)} copy(bf16[512,512]{1,0:T(8,128)(2,1)S(1)} %get-tuple-element.23) | data formatting | bytes 1048576
Async XLA Ops:
  1.5 1.0 %copy-start = (bf16[512,512]{1,0:T(8,128)(2,1)S(1)}, bf16[512,512]{1,0:T(8,128)(2,1)}, u32[]{:S(2)}) copy-start(bf16[512,512]{1,0:T(8,128)(2,1)} %feat_hbm.1) | copy-start | bytes 1572868
  2.6 1.0 %copy-start.1 = (bf16[512,512]{1,0:T(8,128)(2,1)S(1)}, bf16[512,512]{1,0:T(8,128)(2,1)}, u32[]{:S(2)}) copy-start(bf16[512,512]{1,0:T(8,128)(2,1)} %halo_hbm.1) | copy-start | bytes 1572868
  3.6 1.0 %copy-start.2 = (bf16[512,512]{1,0:T(8,128)(2,1)S(1)}, bf16[512,512]{1,0:T(8,128)(2,1)}, u32[]{:S(2)}) copy-start(bf16[512,512]{1,0:T(8,128)(2,1)} %gin_hbm.1) | copy-start | bytes 1572868
  4.7 1.0 %copy-start.3 = (bf16[512,512]{1,0:T(8,128)(2,1)S(1)}, bf16[512,512]{1,0:T(8,128)(2,1)}, u32[]{:S(2)}) copy-start(bf16[512,512]{1,0:T(8,128)(2,1)} %ograd_hbm.1) | copy-start | bytes 1572868
  5.7 1.0 %copy-start.4 = (bf16[512,512]{1,0:T(8,128)(2,1)S(1)}, bf16[512,512]{1,0:T(8,128)(2,1)}, u32[]{:S(2)}) copy-start(bf16[512,512]{1,0:T(8,128)(2,1)} %ws_hbm.1) | copy-start | bytes 1572868
  6.7 1.0 %copy-start.5 = (bf16[512,512]{1,0:T(8,128)(2,1)S(1)}, bf16[512,512]{1,0:T(8,128)(2,1)}, u32[]{:S(2)}) copy-start(bf16[512,512]{1,0:T(8,128)(2,1)} %wn_hbm.1) | copy-start | bytes 1572868
  7.8 0.7 copy-start.6

commit v2 on v1

--- a/solution.py
+++ b/solution.py
@@ -26,10 +26,10 @@
 def kernel(
     scale,
     feat_hbm, halo_hbm, nbr_hbm, send_hbm, gin_hbm, ograd_hbm, ws_hbm, wn_hbm,
-    layer_hbm, fgrad_hbm, nhalo_hbm, nghalo_hbm, wout_hbm,
+    layer, fgrad, nhalo, nghalo, ag,
     table, pair, nbr, send, gin, ograd, wself, wneigh,
-    counts, select, act, layer, fgrad, hgrad, sent,
-    wpart, crecv, s1, xsend, xrecv, s2, ysend, yrecv, zbuf, ag,
+    counts, select, act, hgrad, sent,
+    wpart, crecv, s1, xsend, xrecv, s2, ysend, yrecv, zbuf,
     lsem, osem, cs, cr, xs, xr, ys, yr, zs, zr, ays, ayr, axs, axr, acs, acr, hs, hr, gs, gr,
 ):
     dom = lax.axis_index("dom")
@@ -48,7 +48,8 @@
         return ((z * NY + lax.rem(y + k, NY)) * 2 + core, g)
 
     def at_z(k):
-        return ((lax.rem(z + k, NZ) * NY + y) * 2 + core, g)
+        to = jnp.where(z >= k, k - 1, k)
+        return ((to * NY + y) * 2 + core, g)
 
     barrier = pltpu.get_barrier_semaphore()
     peers = [at_core()] + [at_x(k) for k in range(1, NX)]
@@ -72,21 +73,27 @@
         copy.start()
 
     copies[0].wait()
-    RB = 64
-    ids = lax.broadcasted_iota(jnp.int32, (RB, 2 * ROWS), 1)
-
-    @pl.loop(0, ROWS // RB)
+    one = jnp.full((16, ROWS), 1, jnp.int16)
+    none = jnp.zeros((16, ROWS), jnp.int16)
+    slots = [
+        jnp.broadcast_to(nbr[pl.ds(k, 1), :], (16, ROWS)).astype(jnp.int16) for k in range(FAN)
+    ]
+    ids = lax.broadcasted_iota(jnp.int32, (16, CW), 0)
+    GROUP = 128
+
+    @pl.loop(0, 2 * ROWS // GROUP)
     def _(b):
-        rows = pl.ds(pl.multiple_of(b * RB, RB), RB)
-        block = nbr[rows, :]
-        total = jnp.zeros((RB, 2 * ROWS), F32)
-        for slot in range(FAN):
-            total = total + jnp.where(block[:, slot : slot + 1] == ids, 1.0, 0.0)
-        counts[rows, :] = total.astype(BF16)
+        for part in range(GROUP // 16):
+            first = pl.multiple_of(b * GROUP + part * 16, 16)
+            row_ids = jnp.tile((ids + first).astype(jnp.int16), (1, ROWS // CW))
+            total = none
+            for slot in slots:
+                total = total + jnp.where(slot == row_ids, one, none)
+            counts[pl.ds(first, 16), :] = total.astype(BF16)
 
     for i in (1, 2, 3, 4, 5, 6):
         copies[i].wait()
-    agg = jnp.dot(counts[...], table[...], preferred_element_type=F32) * (1.0 / FAN)
+    agg = lax.dot_general(counts[...], table[...], DIM0, preferred_element_type=F32) * (1.0 / FAN)
     pair[1] = agg.astype(BF16)
     pre = jnp.dot(table[pl.ds(0, ROWS), :], wself[...], preferred_element_type=F32)
     pre = pre + jnp.dot(pair[1], wneigh[...], preferred_element_type=F32)
@@ -115,8 +122,6 @@
     for c in range(CH):
         remote(wpart.at[1, :, cols(c)], crecv.at[:, cols(c)], cs.at[c], cr.at[c], at_core())
     wpart[0] = lax.dot_general(pair[core], act[...], DIM0, preferred_element_type=F32)
-    out_layer = pltpu.make_async_copy(layer, layer_hbm, osem.at[0])
-    out_layer.start()
 
     for c in range(CH):
         wait_for(crecv.at[:, cols(c)], cr.at[c])
@@ -139,8 +144,8 @@
     for k in range(1, NX):
         to = lax.rem(g + k, NX)
         rows = pl.ds(pl.multiple_of(to * XB, XB), XB)
-        remote(sent.at[rows], nhalo_hbm.at[here], hs, hr, at_x(k))
-    own_sent = pltpu.make_async_copy(sent.at[here], nhalo_hbm.at[here], osem.at[1])
+        remote(sent.at[rows], nhalo.at[here], hs, hr, at_x(k))
+    own_sent = pltpu.make_async_copy(sent.at[here], nhalo.at[here], osem.at[0])
     own_sent.start()
 
     for c in range(CH):
@@ -162,15 +167,15 @@
     grad = grad * (1.0 / FAN)
     high = grad.astype(BF16)
     low = (grad - high.astype(F32)).astype(BF16)
-    back = lax.dot_general(
-        counts[:, pl.ds(ROWS, ROWS)], high, DIM0, preferred_element_type=F32
-    ) + lax.dot_general(counts[:, pl.ds(ROWS, ROWS)], low, DIM0, preferred_element_type=F32)
+    halo_counts = counts[pl.ds(ROWS, ROWS), :]
+    back = jnp.dot(halo_counts, high, preferred_element_type=F32)
+    back = back + jnp.dot(halo_counts, low, preferred_element_type=F32)
     hgrad[...] = back.astype(BF16)
     for k in range(1, NX):
         to = lax.rem(g + k, NX)
         rows = pl.ds(pl.multiple_of(to * XB, XB), XB)
-        remote(hgrad.at[rows], nghalo_hbm.at[here], gs, gr, at_x(k))
-    own_grad = pltpu.make_async_copy(hgrad.at[here], nghalo_hbm.at[here], osem.at[2])
+        remote(hgrad.at[rows], nghalo.at[here], gs, gr, at_x(k))
+    own_grad = pltpu.make_async_copy(hgrad.at[here], nghalo.at[here], osem.at[1])
     own_grad.start()
 
     own_y = pl.ds(pl.multiple_of(y * YB, YB), YB)
@@ -185,16 +190,11 @@
             remote(zbuf.at[c, own_z], zbuf.at[c, own_z], zs.at[c], zr.at[c], at_z(k))
 
     own = lax.dot_general(act[...], wself[...], DIM1, preferred_element_type=F32)
-    own = own + lax.dot_general(
-        counts[:, pl.ds(0, ROWS)], high, DIM0, preferred_element_type=F32
-    )
-    own = own + lax.dot_general(
-        counts[:, pl.ds(0, ROWS)], low, DIM0, preferred_element_type=F32
-    )
+    own_counts = counts[pl.ds(0, ROWS), :]
+    own = own + jnp.dot(own_counts, high, preferred_element_type=F32)
+    own = own + jnp.dot(own_counts, low, preferred_element_type=F32)
     own = own + jnp.dot(select[...], gin[...], preferred_element_type=F32)
     fgrad[...] = own.astype(BF16)
-    out_fgrad = pltpu.make_async_copy(fgrad, fgrad_hbm, osem.at[3])
-    out_fgrad.start()
 
     row_y = pl.ds(pl.multiple_of(mine + g * XB + y * YB, YB), YB)
     row_x = pl.ds(pl.multiple_of(mine + g * XB, XB), XB)
@@ -219,15 +219,11 @@
     for c in range(CH):
         wait_for(ag.at[pl.ds(0, (NX - 1) * XB), cols(c)], axr.at[c])
         remote(ag.at[row_c, cols(c)], ag.at[row_c, cols(c)], acs.at[c], acr.at[c], at_core())
-    out_mine = pltpu.make_async_copy(ag.at[row_c], wout_hbm.at[row_c], osem.at[4])
-    out_mine.start()
     for c in range(CH):
         wait_for(ag.at[row_o, cols(c)], acr.at[c])
-    out_other = pltpu.make_async_copy(ag.at[row_o], wout_hbm.at[row_o], osem.at[5])
-    out_other.start()
-
-    wait_for(nhalo_hbm.at[pl.ds(0, ROWS - XB)], hr)
-    wait_for(nghalo_hbm.at[pl.ds(0, ROWS - XB)], gr)
+
+    wait_for(nhalo.at[pl.ds(0, ROWS - XB)], hr)
+    wait_for(nghalo.at[pl.ds(0, ROWS - XB)], gr)
     wait_for(sent.at[pl.ds(0, ROWS - XB)], hs)
     wait_for(hgrad.at[pl.ds(0, ROWS - XB)], gs)
     for c in range(CH):
@@ -238,30 +234,53 @@
         wait_for(ag.at[pl.ds(0, (NY - 1) * YB), cols(c)], ays.at[c])
         wait_for(ag.at[pl.ds(0, (NX - 1) * XB), cols(c)], axs.at[c])
         wait_for(ag.at[row_c, cols(c)], acs.at[c])
-    for copy in (out_layer, own_sent, own_grad, out_fgrad, out_mine, out_other):
+    for copy in (own_sent, own_grad):
+        copy.wait()
+
+
+def deliver(layer, fgrad, nhalo, nghalo, ag, o_layer, o_fgrad, o_nhalo, o_nghalo, o_w, wide, sems, wsems):
+    pairs = ((layer, o_layer), (fgrad, o_fgrad), (nhalo, o_nhalo), (nghalo, o_nghalo))
+    copies = [pltpu.make_async_copy(s, d, sems.at[i]) for i, (s, d) in enumerate(pairs)]
+    for copy in copies:
+        copy.start()
+    pieces = wsems.shape[1]
+    size = ROWS // pieces
+    for m in range(2):
+        for q in range(pieces):
+            rows = pl.ds(q * size, size)
+            wide[m, rows, :] = ag[pl.ds(m * ROWS + q * size, size), :].astype(F32)
+            copies.append(
+                pltpu.make_async_copy(wide.at[m, rows], o_w.at[m, rows], wsems.at[m, q])
+            )
+            copies[-1].start()
+    for copy in copies:
         copy.wait()
 
 
 def body(features, halo_in, neighbors, send_rows, grad_halo_in, out_grad, w_self, w_neigh):
     total_nodes = ROWS * lax.axis_size("dom") * lax.axis_size("grp")
     scale = 1.0 / math.sqrt(total_nodes)
-    rows = jax.ShapeDtypeStruct((ROWS, H), BF16)
-    anywhere = pl.BlockSpec(memory_space=pl.ANY)
+    inside = pl.BlockSpec(memory_space=pltpu.VMEM)
+    outside = pl.BlockSpec(memory_space=pltpu.HBM)
     half = pltpu.VMEM((ROWS, H), BF16)
     dma = pltpu.SemaphoreType.DMA
-    layer_out, feat_grad, next_halo, next_grad_halo, weights = pl.pallas_call(
+    args = [
+        features, halo_in, neighbors.T, send_rows.reshape(1, ROWS), grad_halo_in, out_grad,
+        w_self, w_neigh,
+    ]
+    results = pl.pallas_call(
         functools.partial(kernel, scale),
-        out_shape=(rows, rows, rows, rows, jax.ShapeDtypeStruct((2 * ROWS, H), BF16)),
-        in_specs=[anywhere] * 8,
-        out_specs=(anywhere,) * 5,
+        out_shape=(half, half, half, half, pltpu.VMEM((2 * ROWS, H), BF16)),
+        in_specs=[outside] * 8,
+        out_specs=(inside,) * 5,
         scratch_shapes=[
             pltpu.VMEM((2 * ROWS, H), BF16),
             pltpu.VMEM((2, ROWS, H), BF16),
-            pltpu.VMEM((ROWS, FAN), jnp.int32),
+            pltpu.VMEM((FAN, ROWS), jnp.int32),
             pltpu.VMEM((1, ROWS), jnp.int32),
             half, half, half, half,
-            pltpu.VMEM((ROWS, 2 * ROWS), BF16),
-            half, half, half, half, half, half,
+            pltpu.VMEM((2 * ROWS, ROWS), BF16),
+            half, half, half, half,
             pltpu.VMEM((2, ROWS, H), F32),
             pltpu.VMEM((ROWS, H), F32),
             pltpu.VMEM((ROWS, H), F32),
@@ -271,18 +290,22 @@
             pltpu.VMEM((XB, H), BF16),
             pltpu.VMEM((CH, (NY - 1) * YB, CW), BF16),
             pltpu.VMEM((CH, NZ * YB, CW), BF16),
-            pltpu.VMEM((2 * ROWS, H), BF16),
-            dma((9,)), dma((6,)),
+            dma((9,)), dma((2,)),
         ] + [dma((CH,))] * 14 + [dma] * 4,
         compiler_params=pltpu.CompilerParams(
             collective_id=0, has_side_effects=True, vmem_limit_bytes=48 << 20
         ),
-    )(
-        features, halo_in, neighbors, send_rows.reshape(1, ROWS), grad_halo_in, out_grad,
-        w_self, w_neigh,
-    )
-    w_grads = weights.astype(F32).reshape(2, ROWS, H)
-    return layer_out, feat_grad, next_halo, next_grad_halo, w_grads
+    )(*[pltpu.with_memory_space_constraint(a, pltpu.HBM) for a in args])
+    rows = jax.ShapeDtypeStruct((ROWS, H), BF16)
+    pieces = 4
+    return pl.pallas_call(
+        deliver,
+        out_shape=(rows, rows, rows, rows, jax.ShapeDtypeStruct((2, ROWS, H), F32)),
+        in_specs=[inside] * 5,
+        out_specs=(outside,) * 5,
+        scratch_shapes=[pltpu.VMEM((2, ROWS, H), F32), dma((4,)), dma((2, pieces))],
+        compiler_params=pltpu.CompilerParams(vmem_limit_bytes=16 << 20),
+    )(*[pltpu.with_memory_space_constraint(a, pltpu.VMEM) for a in results])
 
 
 def solution(mesh):

time: 69.4 us -> 55.1 us (0.79)
  local copies, waits for them, and re-layouts: 11 us -> 0 us
  other arithmetic: 2.84 us -> 0 us
    unnamed x19 -> x0, local copies, waits for them, and re-layouts: 11 us -> none
    reshape x1 -> x0, other arithmetic: 2.84 us -> none  [body(): w_grads = weights.astype(F32).reshape(2, ROWS, H)]
    pallas_call x1 -> x2, Pallas kernels: 54.4 us -> 54.3 us  [the longest x1 52.2 us: body(): pl.pallas_call(functools.partial(kernel, scale), out_shape=(half, half, h...]
where the time goes in v2:
time: 55.1 us; the launch traced here: 55 us
  Pallas kernels  54.3 us (99%)
  between operations  0.64 us (1%)
    pallas_call x1, Pallas kernels, body(): pl.pallas_call(functools.partial(kernel, scale), out_shape=(half, half, h...  52.2 us
    pallas_call x1, Pallas kernels, body(): pl.pallas_call(deliver, out_shape=(rows, rows, rows, rows, jax.ShapeDtype...  2.1 us

profile of v2, /device:TPU:1, one launch (start us, length us, event | category | flops | bytes accessed | tf_op | source)
XLA Modules:
  0.0 55.0 jit_solution(4381372195453958961)
XLA Ops:
  0.6 52.2 %shard_map.119 = (bf16[512,512]{1,0:T(8,128)(2,1)S(1)}, bf16[512,512]{1,0:T(8,128)(2,1)S(1)}, bf16[512,512]{1,0:T(8,128)(2,1)S(1)}, bf16[512,512]{1,0:T(8,128)(2,1)S(1)}, bf16[1024,512]{1,0:T(8,128)(2,1)S(1)}) custom-call(bf16[512,512]{1,0:T(8,128)(2,1)} %feat_hbm.1, bf16[512,512]{1,0:T(8,128)(2,1)} %halo_hbm.1, s32[10,512]{1,0:T(8,128)} %bitcast.2, ...), custom_call_target="tpu_custom_call" | custom-call | tf_op jit(solution)/shard_map/pallas_call | solution.py:271
  52.9 2.1 %shard_map.120 = (bf16[512,512]{1,0:T(8,128)(2,1)}, bf16[512,512]{1,0:T(8,128)(2,1)}, bf16[512,512]{1,0:T(8,128)(2,1)}, bf16[512,512]{1,0:T(8,128)(2,1)}, f32[2,512,512]{2,1,0:T(8,128)}) custom-call(bf16[512,512]{1,0:T(8,128)(2,1)S(1)} %get-tuple-element.10.layer, bf16[512,512]{1,0:T(8,128)(2,1)S(1)} %get-tuple-element.11.fgrad, ...), custom_call_target="tpu_custom_call" | custom-call | tf_op jit(solution)/shard_map/pallas_call | solution.py:301

commit v3 on v2

--- a/solution.py
+++ b/solution.py
@@ -16,6 +16,9 @@
 XB = ROWS // NX
 YB = XB // NY
 CH = 4
+FIRST = 2
+FAR_X = (2, 1, 3)
+FAR_Y = (4, 3, 5, 2, 6, 1, 7)
 CW = H // CH
 DIM0 = (((0,), (0,)), ((), ()))
 DIM1 = (((1,), (1,)), ((), ()))
@@ -78,14 +81,14 @@
     slots = [
         jnp.broadcast_to(nbr[pl.ds(k, 1), :], (16, ROWS)).astype(jnp.int16) for k in range(FAN)
     ]
-    ids = lax.broadcasted_iota(jnp.int32, (16, CW), 0)
+    ids = lax.broadcasted_iota(jnp.int32, (16, 128), 0)
     GROUP = 128
 
     @pl.loop(0, 2 * ROWS // GROUP)
     def _(b):
         for part in range(GROUP // 16):
             first = pl.multiple_of(b * GROUP + part * 16, 16)
-            row_ids = jnp.tile((ids + first).astype(jnp.int16), (1, ROWS // CW))
+            row_ids = jnp.tile((ids + first).astype(jnp.int16), (1, ROWS // 128))
             total = none
             for slot in slots:
                 total = total + jnp.where(slot == row_ids, one, none)
@@ -128,7 +131,7 @@
         total = wpart[0, :, cols(c)] + crecv[:, cols(c)]
         s1[:, cols(c)] = total
         xsend[:, cols(c)] = total.astype(BF16)
-        for k in range(1, NX):
+        for k in FAR_X:
             to = lax.rem(g + k, NX)
             rows = pl.ds(pl.multiple_of(to * XB, XB), XB)
             remote(xsend.at[rows, cols(c)], xrecv.at[c, k - 1], xs.at[c], xr.at[c], at_x(k))
@@ -155,7 +158,7 @@
             total = total + xrecv[c, k].astype(F32)
         s2[:, cols(c)] = total
         ysend[:, cols(c)] = total.astype(BF16)
-        for k in range(1, NY):
+        for k in FAR_Y:
             to = lax.rem(y + k, NY)
             rows = pl.ds(pl.multiple_of(to * YB, YB), YB)
             remote(
@@ -186,7 +189,10 @@
         for k in range(NY - 1):
             total = total + yrecv[c, pl.ds(k * YB, YB), :].astype(F32)
         zbuf[c, own_z, :] = total.astype(BF16)
-        for k in range(1, NZ):
+        for k in range(1, FIRST + 1):
+            remote(zbuf.at[c, own_z], zbuf.at[c, own_z], zs.at[c], zr.at[c], at_z(k))
+    for c in range(CH):
+        for k in range(FIRST + 1, NZ):
             remote(zbuf.at[c, own_z], zbuf.at[c, own_z], zs.at[c], zr.at[c], at_z(k))
 
     own = lax.dot_general(act[...], wself[...], DIM1, preferred_element_type=F32)
@@ -206,13 +212,13 @@
         for k in range(1, NZ):
             total = total + zbuf[c, pl.ds(k * YB, YB), :].astype(F32)
         ag[row_y, cols(c)] = (total * scale).astype(BF16)
-        for k in range(1, NY):
+        for k in FAR_Y:
             remote(
                 ag.at[row_y, cols(c)], ag.at[row_y, cols(c)], ays.at[c], ayr.at[c], at_y(k)
             )
     for c in range(CH):
         wait_for(ag.at[pl.ds(0, (NY - 1) * YB), cols(c)], ayr.at[c])
-        for k in range(1, NX):
+        for k in FAR_X:
             remote(
                 ag.at[row_x, cols(c)], ag.at[row_x, cols(c)], axs.at[c], axr.at[c], at_x(k)
             )

time: 55.1 us -> 53.5 us (0.971)
  Pallas kernels: 54.3 us -> 52.8 us
    pallas_call x1, Pallas kernels: 52.2 us -> 50.7 us  [body(): pl.pallas_call(functools.partial(kernel, scale), out_shape=(half, half, h...]
where the time goes in v3:
time: 53.5 us; the launch traced here: 53.4 us
  Pallas kernels  52.8 us (99%)
  between operations  0.64 us (1%)
    pallas_call x1, Pallas kernels, body(): pl.pallas_call(functools.partial(kernel, scale), out_shape=(half, half, h...  50.7 us
    pallas_call x1, Pallas kernels, body(): pl.pallas_call(deliver, out_shape=(rows, rows, rows, rows, jax.ShapeDtype...  2.1 us

profile of v3, /device:TPU:1, one launch (start us, length us, event | category | flops | bytes accessed | tf_op | source)
XLA Modules:
  0.0 53.4 jit_solution(5570676325167446987)
XLA Ops:
  0.6 50.7 %shard_map.119 = (bf16[512,512]{1,0:T(8,128)(2,1)S(1)}, bf16[512,512]{1,0:T(8,128)(2,1)S(1)}, bf16[512,512]{1,0:T(8,128)(2,1)S(1)}, bf16[512,512]{1,0:T(8,128)(2,1)S(1)}, bf16[1024,512]{1,0:T(8,128)(2,1)S(1)}) custom-call(bf16[512,512]{1,0:T(8,128)(2,1)} %feat_hbm.1, bf16[512,512]{1,0:T(8,128)(2,1)} %halo_hbm.1, s32[10,512]{1,0:T(8,128)} %bitcast.2, ...), custom_call_target="tpu_custom_call" | custom-call | tf_op jit(solution)/shard_map/pallas_call | solution.py:277
  51.3 2.1 %shard_map.120 = (bf16[512,512]{1,0:T(8,128)(2,1)}, bf16[512,512]{1,0:T(8,128)(2,1)}, bf16[512,512]{1,0:T(8,128)(2,1)}, bf16[512,512]{1,0:T(8,128)(2,1)}, f32[2,512,512]{2,1,0:T(8,128)}) custom-call(bf16[512,512]{1,0:T(8,128)(2,1)S(1)} %get-tuple-element.10.layer, bf16[512,512]{1,0:T(8,128)(2,1)S(1)} %get-tuple-element.11.fgrad, ...), custom_call_target="tpu_custom_call" | custom-call | tf_op jit(solution)/shard_map/pallas_call | solution.py:307

commit v4 on v3

--- a/solution.py
+++ b/solution.py
@@ -15,11 +15,11 @@
 FAN = 10
 XB = ROWS // NX
 YB = XB // NY
-CH = 4
+WIDTHS = (128, 256, 128)
+CH = len(WIDTHS)
 FIRST = 2
 FAR_X = (2, 1, 3)
 FAR_Y = (4, 3, 5, 2, 6, 1, 7)
-CW = H // CH
 DIM0 = (((0,), (0,)), ((), ()))
 DIM1 = (((1,), (1,)), ((), ()))
 F32 = jnp.float32
@@ -108,7 +108,7 @@
     other = ROWS - mine
 
     def cols(c):
-        return pl.ds(c * CW, CW)
+        return pl.ds(sum(WIDTHS[:c]), WIDTHS[c])
 
     def remote(src, dst, send_sem, recv_sem, device):
         copy = pltpu.make_async_remote_copy(
@@ -120,9 +120,11 @@
     def wait_for(ref, sem):
         pltpu.make_async_copy(ref, ref, sem).wait()
 
-    wpart[1] = lax.dot_general(pair[1 - core], act[...], DIM0, preferred_element_type=F32)
     pl.semaphore_wait(barrier, len(peers))
     for c in range(CH):
+        wpart[1, :, cols(c)] = lax.dot_general(
+            pair[1 - core], act[:, cols(c)], DIM0, preferred_element_type=F32
+        )
         remote(wpart.at[1, :, cols(c)], crecv.at[:, cols(c)], cs.at[c], cr.at[c], at_core())
     wpart[0] = lax.dot_general(pair[core], act[...], DIM0, preferred_element_type=F32)
 
@@ -134,7 +136,7 @@
         for k in FAR_X:
             to = lax.rem(g + k, NX)
             rows = pl.ds(pl.multiple_of(to * XB, XB), XB)
-            remote(xsend.at[rows, cols(c)], xrecv.at[c, k - 1], xs.at[c], xr.at[c], at_x(k))
+            remote(xsend.at[rows, cols(c)], xrecv.at[k - 1, :, cols(c)], xs.at[c], xr.at[c], at_x(k))
 
     copies[7].wait()
     copies[8].wait()
@@ -151,21 +153,6 @@
     own_sent = pltpu.make_async_copy(sent.at[here], nhalo.at[here], osem.at[0])
     own_sent.start()
 
-    for c in range(CH):
-        wait_for(xrecv.at[c], xr.at[c])
-        total = s1[here, cols(c)]
-        for k in range(NX - 1):
-            total = total + xrecv[c, k].astype(F32)
-        s2[:, cols(c)] = total
-        ysend[:, cols(c)] = total.astype(BF16)
-        for k in FAR_Y:
-            to = lax.rem(y + k, NY)
-            rows = pl.ds(pl.multiple_of(to * YB, YB), YB)
-            remote(
-                ysend.at[rows, cols(c)], yrecv.at[c, pl.ds((k - 1) * YB, YB)],
-                ys.at[c], yr.at[c], at_y(k),
-            )
-
     grad = lax.dot_general(act[...], wneigh[...], DIM1, preferred_element_type=F32)
     grad = grad * (1.0 / FAN)
     high = grad.astype(BF16)
@@ -181,19 +168,34 @@
     own_grad = pltpu.make_async_copy(hgrad.at[here], nghalo.at[here], osem.at[1])
     own_grad.start()
 
+    for c in range(CH):
+        wait_for(xrecv.at[:, :, cols(c)], xr.at[c])
+        total = s1[here, cols(c)]
+        for k in range(NX - 1):
+            total = total + xrecv[k, :, cols(c)].astype(F32)
+        s2[:, cols(c)] = total
+        ysend[:, cols(c)] = total.astype(BF16)
+        for k in FAR_Y:
+            to = lax.rem(y + k, NY)
+            rows = pl.ds(pl.multiple_of(to * YB, YB), YB)
+            remote(
+                ysend.at[rows, cols(c)], yrecv.at[pl.ds((k - 1) * YB, YB), cols(c)],
+                ys.at[c], yr.at[c], at_y(k),
+            )
+
     own_y = pl.ds(pl.multiple_of(y * YB, YB), YB)
     own_z = pl.ds(pl.multiple_of(z * YB, YB), YB)
     for c in range(CH):
-        wait_for(yrecv.at[c], yr.at[c])
+        wait_for(yrecv.at[:, cols(c)], yr.at[c])
         total = s2[own_y, cols(c)]
         for k in range(NY - 1):
-            total = total + yrecv[c, pl.ds(k * YB, YB), :].astype(F32)
-        zbuf[c, own_z, :] = total.astype(BF16)
+            total = total + yrecv[pl.ds(k * YB, YB), cols(c)].astype(F32)
+        zbuf[own_z, cols(c)] = total.astype(BF16)
         for k in range(1, FIRST + 1):
-            remote(zbuf.at[c, own_z], zbuf.at[c, own_z], zs.at[c], zr.at[c], at_z(k))
+            remote(zbuf.at[own_z, cols(c)], zbuf.at[own_z, cols(c)], zs.at[c], zr.at[c], at_z(k))
     for c in range(CH):
         for k in range(FIRST + 1, NZ):
-            remote(zbuf.at[c, own_z], zbuf.at[c, own_z], zs.at[c], zr.at[c], at_z(k))
+            remote(zbuf.at[own_z, cols(c)], zbuf.at[own_z, cols(c)], zs.at[c], zr.at[c], at_z(k))
 
     own = lax.dot_general(act[...], wself[...], DIM1, preferred_element_type=F32)
     own_counts = counts[pl.ds(0, ROWS), :]
@@ -207,10 +209,10 @@
     row_c = pl.ds(pl.multiple_of(mine, ROWS), ROWS)
     row_o = pl.ds(pl.multiple_of(other, ROWS), ROWS)
     for c in range(CH):
-        wait_for(zbuf.at[c, pl.ds(0, (NZ - 1) * YB)], zr.at[c])
-        total = zbuf[c, pl.ds(0, YB), :].astype(F32)
+        wait_for(zbuf.at[pl.ds(0, (NZ - 1) * YB), cols(c)], zr.at[c])
+        total = zbuf[pl.ds(0, YB), cols(c)].astype(F32)
         for k in range(1, NZ):
-            total = total + zbuf[c, pl.ds(k * YB, YB), :].astype(F32)
+            total = total + zbuf[pl.ds(k * YB, YB), cols(c)].astype(F32)
         ag[row_y, cols(c)] = (total * scale).astype(BF16)
         for k in FAR_Y:
             remote(
@@ -234,9 +236,9 @@
     wait_for(hgrad.at[pl.ds(0, ROWS - XB)], gs)
     for c in range(CH):
         wait_for(crecv.at[:, cols(c)], cs.at[c])
-        wait_for(xrecv.at[c], xs.at[c])
-        wait_for(yrecv.at[c], ys.at[c])
-        wait_for(zbuf.at[c, pl.ds(0, (NZ - 1) * YB)], zs.at[c])
+        wait_for(xrecv.at[:, :, cols(c)], xs.at[c])
+        wait_for(yrecv.at[:, cols(c)], ys.at[c])
+        wait_for(zbuf.at[pl.ds(0, (NZ - 1) * YB), cols(c)], zs.at[c])
         wait_for(ag.at[pl.ds(0, (NY - 1) * YB), cols(c)], ays.at[c])
         wait_for(ag.at[pl.ds(0, (NX - 1) * XB), cols(c)], axs.at[c])
         wait_for(ag.at[row_c, cols(c)], acs.at[c])
@@ -291,11 +293,11 @@
             pltpu.VMEM((ROWS, H), F32),
             pltpu.VMEM((ROWS, H), F32),
             half,
-            pltpu.VMEM((CH, NX - 1, XB, CW), BF16),
+            pltpu.VMEM((NX - 1, XB, H), BF16),
             pltpu.VMEM((XB, H), F32),
             pltpu.VMEM((XB, H), BF16),
-            pltpu.VMEM((CH, (NY - 1) * YB, CW), BF16),
-            pltpu.VMEM((CH, NZ * YB, CW), BF16),
+            pltpu.VMEM(((NY - 1) * YB, H), BF16),
+            pltpu.VMEM((NZ * YB, H), BF16),
             dma((9,)), dma((2,)),
         ] + [dma((CH,))] * 14 + [dma] * 4,
         compiler_params=pltpu.CompilerParams(

time: 53.5 us -> 53.5 us (level)
  no operation moved by 1% of the time
where the time goes in v4:
time: 53.5 us; the launch traced here: 53.4 us
  Pallas kernels  52.7 us (99%)
  between operations  0.64 us (1%)
    pallas_call x1, Pallas kernels, body(): pl.pallas_call(functools.partial(kernel, scale), out_shape=(half, half, h...  50.6 us
    pallas_call x1, Pallas kernels, body(): pl.pallas_call(deliver, out_shape=(rows, rows, rows, rows, jax.ShapeDtype...  2.1 us

profile of v4, /device:TPU:1, one launch (start us, length us, event | category | flops | bytes accessed | tf_op | source)
XLA Modules:
  0.0 53.4 jit_solution(13771782402112329119)
XLA Ops:
  0.6 50.6 %shard_map.119 = (bf16[512,512]{1,0:T(8,128)(2,1)S(1)}, bf16[512,512]{1,0:T(8,128)(2,1)S(1)}, bf16[512,512]{1,0:T(8,128)(2,1)S(1)}, bf16[512,512]{1,0:T(8,128)(2,1)S(1)}, bf16[1024,512]{1,0:T(8,128)(2,1)S(1)}) custom-call(bf16[512,512]{1,0:T(8,128)(2,1)} %feat_hbm.1, bf16[512,512]{1,0:T(8,128)(2,1)} %halo_hbm.1, s32[10,512]{1,0:T(8,128)} %bitcast.2, ...), custom_call_target="tpu_custom_call" | custom-call | tf_op jit(solution)/shard_map/pallas_call | solution.py:279
  51.3 2.1 %shard_map.120 = (bf16[512,512]{1,0:T(8,128)(2,1)}, bf16[512,512]{1,0:T(8,128)(2,1)}, bf16[512,512]{1,0:T(8,128)(2,1)}, bf16[512,512]{1,0:T(8,128)(2,1)}, f32[2,512,512]{2,1,0:T(8,128)}) custom-call(bf16[512,512]{1,0:T(8,128)(2,1)S(1)} %get-tuple-element.10.layer, bf16[512,512]{1,0:T(8,128)(2,1)S(1)} %get-tuple-element.11.fgrad, ...), custom_call_target="tpu_custom_call" | custom-call | tf_op jit(solution)/shard_map/pallas_call | solution.py:309

commit v5 on v4

--- a/solution.py
+++ b/solution.py
@@ -57,9 +57,6 @@
     barrier = pltpu.get_barrier_semaphore()
     peers = [at_core()] + [at_x(k) for k in range(1, NX)]
     peers += [at_y(k) for k in range(1, NY)] + [at_z(k) for k in range(1, NZ)]
-    for peer in peers:
-        pl.semaphore_signal(barrier, inc=1, device_id=peer, device_id_type=MESH)
-
     loads = [
         (nbr_hbm, nbr),
         (feat_hbm, table.at[pl.ds(0, ROWS)]),
@@ -74,6 +71,8 @@
     copies = [pltpu.make_async_copy(s, d, lsem.at[i]) for i, (s, d) in enumerate(loads)]
     for copy in copies:
         copy.start()
+    for peer in peers:
+        pl.semaphore_signal(barrier, inc=1, device_id=peer, device_id_type=MESH)
 
     copies[0].wait()
     one = jnp.full((16, ROWS), 1, jnp.int16)

time: 53.5 us -> 53.6 us (level)
  no operation moved by 1% of the time
where the time goes in v5:
time: 53.6 us; the launch traced here: 53.4 us
  Pallas kernels  52.8 us (99%)
  between operations  0.64 us (1%)
    pallas_call x1, Pallas kernels, body(): pl.pallas_call(functools.partial(kernel, scale), out_shape=(half, half, h...  50.7 us
    pallas_call x1, Pallas kernels, body(): pl.pallas_call(deliver, out_shape=(rows, rows, rows, rows, jax.ShapeDtype...  2.1 us

profile of v5, /device:TPU:1, one launch (start us, length us, event | category | flops | bytes accessed | tf_op | source)
XLA Modules:
  0.0 53.4 jit_solution(7976749685040944300)
XLA Ops:
  0.6 50.7 %shard_map.119 = (bf16[512,512]{1,0:T(8,128)(2,1)S(1)}, bf16[512,512]{1,0:T(8,128)(2,1)S(1)}, bf16[512,512]{1,0:T(8,128)(2,1)S(1)}, bf16[512,512]{1,0:T(8,128)(2,1)S(1)}, bf16[1024,512]{1,0:T(8,128)(2,1)S(1)}) custom-call(bf16[512,512]{1,0:T(8,128)(2,1)} %feat_hbm.1, bf16[512,512]{1,0:T(8,128)(2,1)} %halo_hbm.1, s32[10,512]{1,0:T(8,128)} %bitcast.2, ...), custom_call_target="tpu_custom_call" | custom-call | tf_op jit(solution)/shard_map/pallas_call | solution.py:278
  51.3 2.1 %shard_map.120 = (bf16[512,512]{1,0:T(8,128)(2,1)}, bf16[512,512]{1,0:T(8,128)(2,1)}, bf16[512,512]{1,0:T(8,128)(2,1)}, bf16[512,512]{1,0:T(8,128)(2,1)}, f32[2,512,512]{2,1,0:T(8,128)}) custom-call(bf16[512,512]{1,0:T(8,128)(2,1)S(1)} %get-tuple-element.10.layer, bf16[512,512]{1,0:T(8,128)(2,1)S(1)} %get-tuple-element.11.fgrad, ...), custom_call_target="tpu_custom_call" | custom-call | tf_op jit(solution)/shard_map/pallas_call | solution.py:308
